TPU v7x, 512 devices: a whole 4x8x8 slice. The times are simulated.
512 devices in a mesh: ctx: 64 (over z_lo, y, x), work: 8 (over z_hi, core).
Axes of the slice: x: 4, y: 8, z: 8 (z_hi: 4, z_lo: 2; z = z_hi * 2 + z_lo), core: 2. Of those that a mesh axis runs over, the one named last changes fastest.
Arguments:
- inputs: bfloat16 [8, 16384, 2880], P('work', 'ctx'), may hold values from -6 to 6
- queries: bfloat16 [8, 16384, 2048], P('work', 'ctx')
- keys: bfloat16 [8, 16384, 256], P('work', 'ctx')
- out_grad: bfloat16 [8, 16384, 2048], P('work', 'ctx'), may hold values from -6 to 6
- positions: int32 [8, 16384], P('work', 'ctx'), may hold values from 0 to 16383, as said below
- bands: int32 [32], replicated, may hold values from 32 to 128, as said below
- step: int32 [1], replicated, may hold values from 1 to 16
- value_weight: float32 [8, 2880, 256], P('work', 'ctx'), may hold values from -0.109375 to 0.109375
- moment_one: float32 [8, 2880, 256], P('work', 'ctx'), may hold values from -0.0078125 to 0.0078125
- moment_two: float32 [8, 2880, 256], P('work', 'ctx'), may hold values from 1e-08 to 1e-06
Outputs:
- attn_out: bfloat16 [8, 16384, 2048], P('work', 'ctx')
- mean_weight: float32 [2880, 256], P('ctx')
- mean_one: float32 [2880, 256], P('ctx')
- mean_two: float32 [2880, 256], P('ctx')
Inputs may be any that keep to these rules, and one draw needn't show every extreme that they name: `positions`: in each worker's sequence a token's position is 0 at the first token and at each document start, else one more than the previous token's. One worker's sequence is a single document. `bands`: one head has exactly 128.
All inputs are finite; a program needn't handle non-finite values.
Results may differ from a plain program's by a relative error of at most 0.0015.
The roundings to bfloat16 on the way count: a program that leaves them out, or rounds other values in their place, can miss the bound.
Values may be sent and summed in bfloat16 or wider, within the bound.
A program may use at most 64 MiB of HBM per device.

v0:
```python
import jax
import jax.numpy as jnp
from jax import lax
from jax.sharding import PartitionSpec as P

HD = 64
QH = 32
KH = 4
LOOKBACK_SPAN = 128


beta_one = 0.9
beta_two = 0.95
adam_eps = 1e-08
learn_rate = 0.01
clip_norm = 0.5


def from_everyone(array, axis):
    copies = jnp.broadcast_to(array, (lax.axis_size(axis), *array.shape))
    return lax.all_to_all(copies, axis, split_axis=0, concat_axis=0, tiled=True)


def joined_along(blocks, dim):
    dims = list(blocks.shape[1:])
    dims[dim] *= blocks.shape[0]
    return jnp.moveaxis(blocks, 0, dim).reshape(dims)


def collect(array, axis, dim):
    blocks = from_everyone(array, axis)
    return joined_along(blocks, dim)


def shifted(array, axis, by):
    devices = lax.axis_size(axis)
    pairs = [(i, i + by) for i in range(devices) if 0 <= i + by < devices]
    return lax.ppermute(array, axis, pairs)


def cut_along(array, dim, devices):
    before, after = (array.shape[:dim], array.shape[dim + 1 :])
    return jnp.moveaxis(array.reshape(*before, devices, -1, *after), dim, 0)


def sent_and_summed(array, axis, dim):
    blocks = cut_along(array, dim, lax.axis_size(axis))
    arrived = lax.all_to_all(blocks, axis, split_axis=0, concat_axis=0, tiled=True)
    return arrived.sum(axis=0)


def taken_together(array, axis):
    return from_everyone(array, axis).sum(axis=0)


def together(arrays, axis):
    flat, at, gathered = (jnp.concatenate([a.reshape(-1) for a in arrays]), 0, [])
    subtotal = taken_together(flat, axis)
    for a in arrays:
        gathered.append(subtotal[at : at + a.size].reshape(a.shape))
        at += a.size
    return tuple(gathered)


def attend(qrows, krows, vrows, grows, bands, pos):
    count = qrows.shape[0]
    span = krows.shape[0]
    halo = span - count
    group = QH // KH
    dist = (
        lax.broadcasted_iota(jnp.int32, (count, span), 0)
        + halo
        - lax.broadcasted_iota(jnp.int32, (count, span), 1)
    )
    near = (dist >= 0) & (dist <= pos[:, None])
    outputs = []
    grads = []
    for head in range(KH):
        lo = head * group * HD
        hi = (head + 1) * group * HD
        query = qrows[:, lo:hi].reshape(count, group, HD)
        keyed = krows[:, head * HD : (head + 1) * HD]
        valued = vrows[:, head * HD : (head + 1) * HD]
        cotan = grows[:, lo:hi].reshape(count, group, HD)
        limit = bands[head * group : (head + 1) * group]
        allowed = near[None] & (dist[None] <= limit[:, None, None])
        scores = jnp.einsum(
            "qgd,kd->gqk", query, keyed, preferred_element_type=jnp.float32
        ) * HD ** (-0.5)
        scores = jnp.where(allowed, scores, -1e30)
        top = jnp.max(scores, axis=2, keepdims=True)
        expo = jnp.exp(scores - top)
        probs = (expo / jnp.sum(expo, axis=2, keepdims=True)).astype(jnp.bfloat16)
        outputs.append(
            jnp.einsum("gqk,kd->qgd", probs, valued, preferred_element_type=jnp.float32).reshape(
                count, group * HD
            )
        )
        grads.append(jnp.einsum("gqk,qgd->kd", probs, cotan, preferred_element_type=jnp.float32))
    return (jnp.concatenate(outputs, 1).astype(jnp.bfloat16), jnp.concatenate(grads, 1))


def per_device(
    inputs, queries, keys, out_grad, positions, bands, step, value_weight, moment_one, moment_two
):
    acts = inputs[0]
    rows = acts.shape[0]
    tokens_all = rows * lax.axis_size("ctx")
    weight = value_weight[0]
    columns = acts
    value_vectors = jnp.dot(
        columns, collect(weight.astype(jnp.bfloat16), "ctx", 0), preferred_element_type=jnp.float32
    ).astype(jnp.bfloat16)
    keyed = keys[0]
    prev_keys, prev_values = shifted(
        (keyed[rows - LOOKBACK_SPAN :], value_vectors[rows - LOOKBACK_SPAN :]), "ctx", 1
    )
    all_keys = jnp.concatenate([prev_keys, keyed], 0)
    all_values = jnp.concatenate([prev_values, value_vectors], 0)
    out, grad_rows = attend(queries[0], all_keys, all_values, out_grad[0], bands, positions[0])
    returned = shifted(grad_rows[:LOOKBACK_SPAN], "ctx", -1)
    own = grad_rows[LOOKBACK_SPAN:]
    own = jnp.concatenate([own[: rows - LOOKBACK_SPAN], own[rows - LOOKBACK_SPAN :] + returned], 0)
    value_grad = own.astype(jnp.bfloat16)
    columns = acts
    grad = (
        sent_and_summed(
            lax.dot_general(
                columns, value_grad, (((0,), (0,)), ((), ())), preferred_element_type=jnp.float32
            ),
            "ctx",
            0,
        )
        / tokens_all
    )
    norm = jnp.sqrt(taken_together(jnp.sum(grad * grad), "ctx"))
    grad = grad * jnp.minimum(1.0, clip_norm / (norm + 1e-06))
    first = beta_one * moment_one[0] + (1.0 - beta_one) * grad
    second = beta_two * moment_two[0] + (1.0 - beta_two) * grad * grad
    count = step[0].astype(jnp.float32)
    fix_one = 1.0 - jnp.power(jnp.float32(beta_one), count)
    fix_two = 1.0 - jnp.power(jnp.float32(beta_two), count)
    updated = weight - learn_rate * (first / fix_one) / (jnp.sqrt(second / fix_two) + adam_eps)
    workers = lax.axis_size("work")
    mean_weight, mean_one, mean_two = together((updated, first, second), "work")
    return (out[None], mean_weight / workers, mean_one / workers, mean_two / workers)


def solution(mesh):
    in_specs = (
        P("work", "ctx", None),
        P("work", "ctx", None),
        P("work", "ctx", None),
        P("work", "ctx", None),
        P("work", "ctx"),
        P(),
        P(),
        P("work", "ctx", None),
        P("work", "ctx", None),
        P("work", "ctx", None),
    )
    out_specs = (P("work", "ctx", None), P("ctx", None), P("ctx", None), P("ctx", None))
    return jax.shard_map(
        per_device, mesh=mesh, in_specs=in_specs, out_specs=out_specs, check_vma=False
    )
```

profile of v0, /device:TPU:1, one launch (start us, length us, event | category | flops | bytes accessed | tf_op | source)
XLA Modules:
  0.0 260.3 jit_solution(6278662177778643547)
XLA Ops:
  2.5 4.6 %collective-permute-start.1 = (bf16[128,256]{0,1:T(8,128)(2,1)}, bf16[128,256]{0,1:T(8,128)(2,1)}, u32[]{:S(2)}, u32[]{:S(2)}) collective-permute-start(bf16[128,256]{0,1:T(8,128)(2,1)} %slice_bitcast_fusion), channel_id=1, source_target_pairs={{0,8},{8,16},{16,24},{24,32},{32,40},{40,48},{48,56},{56,64},{64,7... | collective-permute-start | bytes 196616 | tf_op jit(solution)/shard_map/ppermute | solution.py:38
  8.6 2.1 fusion.108
  22.3 3.8 %fusion.115 = (f32[8,256]{1,0:T(8,128)S(1)}, f32[8,256,384]{1,2,0:T(8,128)}) fusion(s32[256,384]{0,1:T(8,128)S(1)} %copy-done.9, s32[8]{0:T(128)S(1)} %get-tuple-element.21, pred[256,384]{0,1:T(8,128)(4,1)S(1)} %compare_and_fusion, bf16[256,8,64]{0,2,1:T(8,128)(2,1)S(1)} %bitcast.153, bf16[256,256]{0,1:T(8,128)(2,1)S(1)} %bitcast.146, ...), kind=kOutput, calls=%fused_computation.139 | convolution fusion | flops 105480576 | bytes 4104224 | tf_op jit(solution)/shard_map/sub | solution.py:92
  26.1 2.2 divide_convert_fusion.2
  28.9 4.2 %fusion.112 = (f32[8,256]{1,0:T(8,128)S(1)}, f32[8,256,384]{1,2,0:T(8,128)}) fusion(s32[256,384]{0,1:T(8,128)} %iota_subtract_fusion, s32[8]{0:T(128)} %get-tuple-element.23, pred[256,384]{0,1:T(8,128)(4,1)} %copy-done.12, bf16[256,8,64]{0,2,1:T(8,128)(2,1)} %bitcast.152, bf16[256,256]{0,1:T(8,128)(2,1)S(1)} %bitcast.147, ...), kind=kOutput, calls=%fused_computation.138 | convolution fusion | flops 105480576 | bytes 4104224 | tf_op jit(solution)/shard_map/sub | solution.py:92
  33.1 2.2 divide_convert_fusion.1
  37.0 4.2 %fusion.111 = (f32[8,256]{1,0:T(8,128)S(1)}, f32[8,256,384]{1,2,0:T(8,128)}) fusion(s32[256,384]{0,1:T(8,128)} %iota_subtract_fusion, s32[8]{0:T(128)S(1)} %get-tuple-element.22, pred[256,384]{0,1:T(8,128)(4,1)} %copy-done.12, bf16[256,8,64]{0,2,1:T(8,128)(2,1)} %bitcast.151, bf16[256,256]{0,1:T(8,128)(2,1)} %bitcast.148, ...), kind=kOutput, calls=%fused_computation.137 | convolution fusion | flops 105480576 | bytes 4104224 | tf_op jit(solution)/shard_map/sub | solution.py:92
  41.2 2.2 divide_convert_fusion
  45.9 4.2 %fusion.118 = (f32[8,256]{1,0:T(8,128)S(1)}, f32[8,256,384]{1,2,0:T(8,128)}) fusion(s32[256,384]{0,1:T(8,128)} %iota_subtract_fusion, s32[8]{0:T(128)S(1)} %get-tuple-element.20, pred[256,384]{0,1:T(8,128)(4,1)} %copy-done.12, bf16[256,8,64]{0,2,1:T(8,128)(2,1)} %bitcast.150, bf16[256,256]{0,1:T(8,128)(2,1)} %bitcast.149, ...), kind=kOutput, calls=%fused_computation.140 | convolution fusion | flops 105480576 | bytes 4104224 | tf_op jit(solution)/shard_map/sub | solution.py:92
  50.0 2.2 divide_convert_fusion.3
  55.4 4.4 %collective-permute-done.2 = f32[128,256]{0,1:T(8,128)S(1)} collective-permute-done((f32[128,256]{0,1:T(8,128)S(1)}, f32[128,256]{0,1:T(8,128)S(1)}, u32[]{:S(2)}, u32[]{:S(2)}) %collective-permute-start.2) | collective-permute-done | bytes 131104 | tf_op jit(solution)/shard_map/ppermute | solution.py:38
  59.8 2.2 convolution_bitcast_fusion
  62.0 4.1 %reshape.233 = f32[64,45,256]{2,1,0:T(8,128)} reshape(f32[2880,256]{1,0:T(8,128)} %convolution_bitcast_fusion) | data formatting | bytes 5898240 | tf_op jit(solution)/shard_map/reshape | solution.py:43
  66.1 84.1 %all_to_all.22 = f32[64,45,256]{2,1,0:T(8,128)} all-to-all(f32[64,45,256]{2,1,0:T(8,128)} %reshape.233), channel_id=1, replica_groups=mesh['ctx'=64,'work'=8] {'ctx'}, dimensions={0} | all-to-all | bytes 5898240 | tf_op jit(solution)/shard_map/all_to_all | solution.py:48
  154.2 7.1 %all-to-all-start.2 = ((f32[64,1,1]{2,1,0:T(1,128)}), f32[64,1,1]{2,1,0:T(1,128)S(1)}, u32[]{:S(2)}, u32[]{:S(2)}) async-start(f32[64,1,1]{2,1,0:T(1,128)} %broadcast_in_dim.15), calls=%async_computation.2 | async-start | bytes 65536 | tf_op jit(solution)/shard_map/all_to_all | solution.py:21
  161.5 9.2 %all-to-all-done.2 = f32[64,1,1]{2,1,0:T(1,128)S(1)} async-done(((f32[64,1,1]{2,1,0:T(1,128)}), f32[64,1,1]{2,1,0:T(1,128)S(1)}, u32[]{:S(2)}, u32[]{:S(2)}) %all-to-all-start.2) | async-done | bytes 288 | tf_op jit(solution)/shard_map/all_to_all | solution.py:21
  171.9 5.5 %all-to-all-start = ((bf16[64,45,256]{2,1,0:T(8,128)(2,1)}), bf16[64,45,256]{2,1,0:T(8,128)(2,1)}, u32[]{:S(2)}, u32[]{:S(2)}) async-start(bf16[64,45,256]{2,1,0:T(8,128)(2,1)} %broadcast_in_dim.13), calls=%async_computation | async-start | bytes 3145728 | tf_op jit(solution)/shard_map/all_to_all | solution.py:21
  180.0 31.6 %all-to-all-done = bf16[64,45,256]{2,1,0:T(8,128)(2,1)} async-done(((bf16[64,45,256]{2,1,0:T(8,128)(2,1)}), bf16[64,45,256]{2,1,0:T(8,128)(2,1)}, u32[]{:S(2)}, u32[]{:S(2)}) %all-to-all-start) | async-done | bytes 1474592 | tf_op jit(solution)/shard_map/all_to_all | solution.py:21
  213.1 15.3 %all-to-all-start.3 = ((f32[8,1,34560]{2,1,0:T(1,128)}), f32[8,1,34560]{2,1,0:T(1,128)}, u32[]{:S(2)}, u32[]{:S(2)}) async-start(f32[8,1,34560]{2,1,0:T(1,128)} %broadcast_in_dim.16), calls=%async_computation.3 | async-start | bytes 2211840 | tf_op jit(solution)/shard_map/all_to_all | solution.py:21
  228.5 3.4 %reshape.224 = bf16[2880,256]{1,0:T(8,128)(2,1)} reshape(bf16[64,45,256]{2,1,0:T(8,128)(2,1)} %all-to-all-done) | data formatting | bytes 2949120 | tf_op jit(solution)/shard_map/reshape | solution.py:27
  233.9 2.4 collective-permute-start
  240.2 2.5 convolution_convert_fusion.1
  244.6 2.6 convolution_convert_fusion
  253.3 3.0 %all-to-all-done.3 = f32[8,1,34560]{2,1,0:T(1,128)} async-done(((f32[8,1,34560]{2,1,0:T(1,128)}), f32[8,1,34560]{2,1,0:T(1,128)}, u32[]{:S(2)}, u32[]{:S(2)}) %all-to-all-start.3) | async-done | bytes 1105952 | tf_op jit(solution)/shard_map/all_to_all | solution.py:21
  (91 shorter events, 48.6 us)
Async XLA Ops:
  0.6 59.1 %copy-start = (bf16[1,256,2880]{1,2,0:T(8,128)(2,1)S(1)}, bf16[1,256,2880]{1,2,0:T(8,128)(2,1)}, u32[]{:S(2)}) copy-start(bf16[1,256,2880]{1,2,0:T(8,128)(2,1)} %param.10) | copy-start | bytes 4423684
  0.6 10.1 %copy-start.5 = (bf16[1,256,2048]{2,1,0:T(8,128)(2,1)S(1)}, bf16[1,256,2048]{2,1,0:T(8,128)(2,1)}, u32[]{:S(2)}) copy-start(bf16[1,256,2048]{2,1,0:T(8,128)(2,1)} %param.13) | copy-start | bytes 3145732
  0.7 11.0 %copy-start.16 = (s32[32]{0:T(128)S(1)}, s32[32]{0:T(128)}, u32[]{:S(2)}) copy-start(s32[32]{0:T(128)} %param.15) | copy-start | bytes 388
  1.8 27.1 %copy-start.11 = (bf16[1,256,256]{1,2,0:T(8,128)(2,1)}, bf16[1,256,256]{1,2,0:T(8,128)(2,1)S(1)}, u32[]{:S(2)}) copy-start(bf16[1,256,256]{1,2,0:T(8,128)(2,1)S(1)} %copy.92) | copy-start | bytes 393220
  2.5 19.8 %collective-permute-start.1 = (bf16[128,256]{0,1:T(8,128)(2,1)}, bf16[128,256]{0,1:T(8,128)(2,1)}, u32[]{:S(2)}, u32[]{:S(2)}) collective-permute-start(bf16[128,256]{0,1:T(8,128)(2,1)} %slice_bitcast_fusion), channel_id=1, source_target_pairs={{0,8},{8,16},{16,24},{24,32},{32,40},{40,48},{48,56},{56,64},{64,7... | collective-permute-start | bytes 196616 | tf_op jit(solution)/shard_map/ppermute | solution.py:38
  8.6 13.7 %copy-start.12 = (pred[256,384]{0,1:T(8,128)(4,1)}, pred[256,384]{0,1:T(8,128)(4,1)S(1)}, u32[]{:S(2)}) copy-start(pred[256,384]{0,1:T(8,128)(4,1)S(1)} %compare_and_fusion) | copy-start | bytes 294916
  11.7 10.7 %copy-start.9 = (s32[256,384]{0,1:T(8,128)S(1)}, s32[256,384]{0,1:T(8,128)}, u32[]{:S(2)}) copy-start(s32[256,384]{0,1:T(8,128)} %iota_subtract_fusion) | copy-start | bytes 1179652
  26.1 2.2 copy-start.8
  33.1 3.4 %copy-start.7 = (bf16[256,512]{0,1:T(8,128)(2,1)S(1)}, bf16[256,512]{0,1:T(8,128)(2,1)}, u32[]{:S(2)}) copy-start(bf16[256,512]{0,1:T(8,128)(2,1)} %copy.114) | copy-start | bytes 786436
  35.3 1.1 copy-start.1
  41.2 3.4 %copy-start.6 = (bf16[256,512]{0,1:T(8,128)(2,1)S(1)}, bf16[256,512]{0,1:T(8,128)(2,1)}, u32[]{:S(2)}) copy-start(bf16[256,512]{0,1:T(8,128)(2,1)} %copy.116) | copy-start | bytes 786436
  43.4 1.2 copy-start.2
  50.0 4.0 %copy-start.10 = (f32[384,64]{0,1:T(8,128)S(1)}, f32[384,64]{0,1:T(8,128)}, u32[]{:S(2)}) copy-start(f32[384,64]{0,1:T(8,128)} %convolution_bitcast_fusion.1) | copy-start | bytes 294916
  52.2 1.2 copy-start.3
  54.0 5.7 %collective-permute-start.2 = (f32[128,256]{0,1:T(8,128)S(1)}, f32[128,256]{0,1:T(8,128)S(1)}, u32[]{:S(2)}, u32[]{:S(2)}) collective-permute-start(f32[128,256]{0,1:T(8,128)S(1)} %slice.168), channel_id=1, source_target_pairs={{8,0},{16,8},{24,16},{32,24},{40,32},{48,40},{56,48},{64,56},{72,6... | collective-permute-start | bytes 393224 | tf_op jit(solution)/shard_map/ppermute | solution.py:38
  150.2 11.2 %copy-start.13 = (f32[1,45,256]{2,0,1:T(1,128)S(1)}, f32[1,45,256]{2,0,1:T(1,128)}, u32[]{:S(2)}) copy-start(f32[1,45,256]{2,0,1:T(1,128)} %param.17) | copy-start | bytes 138244
  152.3 25.9 %copy-start.14 = (f32[1,45,256]{2,0,1:T(1,128)S(1)}, f32[1,45,256]{2,0,1:T(1,128)}, u32[]{:S(2)}) copy-start(f32[1,45,256]{2,0,1:T(1,128)} %param.18) | copy-start | bytes 138244
  152.3 26.0 %copy-start.15 = (f32[1,45,256]{2,0,1:T(1,128)S(1)}, f32[1,45,256]{2,0,1:T(1,128)}, u32[]{:S(2)}) copy-start(f32[1,45,256]{2,0,1:T(1,128)} %param.19) | copy-start | bytes 138244
  154.2 16.5 %all-to-all-start.2 = ((f32[64,1,1]{2,1,0:T(1,128)}), f32[64,1,1]{2,1,0:T(1,128)S(1)}, u32[]{:S(2)}, u32[]{:S(2)}) async-start(f32[64,1,1]{2,1,0:T(1,128)} %broadcast_in_dim.15), calls=%async_computation.2 | async-start | bytes 65536 | tf_op jit(solution)/shard_map/all_to_all | solution.py:21
  171.9 39.7 %all-to-all-start = ((bf16[64,45,256]{2,1,0:T(8,128)(2,1)}), bf16[64,45,256]{2,1,0:T(8,128)(2,1)}, u32[]{:S(2)}, u32[]{:S(2)}) async-start(bf16[64,45,256]{2,1,0:T(8,128)(2,1)} %broadcast_in_dim.13), calls=%async_computation | async-start | bytes 3145728 | tf_op jit(solution)/shard_map/all_to_all | solution.py:21
  213.1 43.1 %all-to-all-start.3 = ((f32[8,1,34560]{2,1,0:T(1,128)}), f32[8,1,34560]{2,1,0:T(1,128)}, u32[]{:S(2)}, u32[]{:S(2)}) async-start(f32[8,1,34560]{2,1,0:T(1,128)} %broadcast_in_dim.16), calls=%async_computation.3 | async-start | bytes 2211840 | tf_op jit(solution)/shard_map/all_to_all | solution.py:21
  233.9 3.9 %collective-permute-start = (bf16[128,256]{1,0:T(8,128)(2,1)S(1)}, bf16[128,256]{1,0:T(8,128)(2,1)S(1)}, u32[]{:S(2)}, u32[]{:S(2)}) collective-permute-start(bf16[128,256]{1,0:T(8,128)(2,1)S(1)} %slice.144), channel_id=1, source_target_pairs={{0,8},{8,16},{16,24},{24,32},{32,40},{40,48},{48,56},{56,64},{64,7... | collective-permute-start | bytes 196616 | tf_op jit(solution)/shard_map/ppermute | solution.py:38
  239.0 9.9 %copy-start.4 = (bf16[8,256,384]{1,2,0:T(8,128)(2,1)S(1)}, bf16[8,256,384]{1,2,0:T(8,128)(2,1)}, u32[]{:S(2)}) copy-start(bf16[8,256,384]{1,2,0:T(8,128)(2,1)} %copy-done.3) | copy-start | bytes 4718596
where the time goes:
time: 264 us; the launch traced here: 260 us
  blocking collectives  84.1 us (32%)
  waiting for transfers between devices  49.7 us (19%)
  local copies, waits for them, and re-layouts  38.5 us (15%)
  starting transfers between devices  36.2 us (14%)
  matrix products  30.8 us (12%)
  other arithmetic  18.4 us (7%)
    all_to_all x1, blocking collectives, sent_and_summed(): lax.all_to_all(blocks, axis, split_axis=0, concat_axis=0, tiled=True)  84.1 us
    all_to_all x3, waiting for transfers between devices, from_everyone(): return lax.all_to_all(copies, axis, split_axis=0, concat_axis=0, tiled=True)  43.8 us
    all_to_all x3, starting transfers between devices, from_everyone(): return lax.all_to_all(copies, axis, split_axis=0, concat_axis=0, tiled=True)  28 us
    sub x4, matrix products, attend(): expo = jnp.exp(scores - top)  16.2 us
    convert_element_type x4, other arithmetic, attend(): probs = (expo / jnp.sum(expo, axis=2, keepdims=True)).astype(jnp.bfloat16)  8.77 us
    ppermute x3, starting transfers between devices, shifted(): return lax.ppermute(array, axis, pairs)  8.25 us
    slice x5, local copies, waits for them, and re-layouts, attend(): query = qrows[:, lo:hi].reshape(count, group, HD)  7.68 us
    dot_general x4, matrix products, attend(): jnp.einsum('gqk,kd->qgd', probs, valued, preferred_element_type=jnp.float32)  7.42 us
  transfers between devices with their start and end apart: 6, of which 5 were waited for; matrix products, arithmetic and copies ran while one was open for 14% of the time, Pallas kernels for 0%

commit v1 on v0

v1 whole, which is shorter than its diff:
```python
import functools
import math

import jax
import jax.numpy as jnp
import numpy as np
from jax import lax
from jax.experimental import pallas as pl
from jax.experimental.pallas import tpu as pltpu
from jax.sharding import PartitionSpec as P

D = 2880
HD = 64
QH = 32
KH = 4
SPAN = 128
ROWS = 256
NZ, NY, NX = 2, 8, 4
NCTX = NZ * NY * NX
NH = 4
NW = 8
OWN = D // NCTX
PAD = 48
TILES = NCTX * PAD // 128

beta_one = 0.9
beta_two = 0.95
adam_eps = 1e-08
learn_rate = 0.01
clip_norm = 0.5

F32 = jnp.float32
BF16 = jnp.bfloat16


def window(tile):
    lane = tile * 128
    source = OWN * (lane // PAD) + min(lane % PAD, OWN - 1)
    low = source // 128 * 128
    return low, min(256, D - low)


def spread_matrix():
    out = np.zeros((TILES, 128, 256), np.float32)
    for tile in range(TILES):
        low, width = window(tile)
        for lane in range(128):
            chunk, row = divmod(tile * 128 + lane, PAD)
            if row < OWN:
                at = chunk * OWN + row - low
                assert 0 <= at < width
                out[tile, lane, at] = 1
    return out


def ring_plan(n):
    plan = []
    for way in (1, -1):
        for half in (0, 1):
            far = n // 2 if (way == 1) == (half == 0) else n // 2 - 1
            plan.append((way, half, far))
    return plan


class Ring:
    def __init__(self, n, at, view, landing, send_sem, recv_sem, first_sem, to):
        self.n, self.at, self.view, self.landing = n, at, view, landing
        self.send_sem, self.recv_sem, self.to = send_sem, recv_sem, to
        self.slots = {}
        slot = 0
        for way, half, far in ring_plan(n):
            for step in range(far):
                self.slots[way, half, step] = (slot, first_sem + slot)
                slot += 1
        self.copies = {}

    def step(self, count):
        for longest in (True, False):
            for way, half, far in ring_plan(self.n):
                step = count
                if (far == self.n // 2) != longest or step > far:
                    continue
                left = far - step
                target = lax.rem(self.at + way * left + self.n, self.n)
                mine = self.view(target, half)
                if step > 0:
                    self.copies[way, half, step - 1].wait_recv()
                    slot, _ = self.slots[way, half, step - 1]
                    mine[...] = mine[...] + self.landing.at[slot][...]
                if left > 0:
                    slot, sem = self.slots[way, half, step]
                    copy = pltpu.make_async_remote_copy(
                        src_ref=mine,
                        dst_ref=self.landing.at[slot],
                        send_sem=self.send_sem.at[sem],
                        recv_sem=self.recv_sem.at[sem],
                        device_id=self.to(way),
                        device_id_type=pl.DeviceIdType.MESH,
                    )
                    copy.start()
                    self.copies[way, half, step] = copy

    def finish(self):
        for copy in self.copies.values():
            copy.wait_send()


def kernel(
    acts, queries, keys, out_grad, positions, bands, step, weight, one, two, spread,
    out, mean_weight, mean_one, mean_two,
    acts_pad, acts_t, k2, v2, probs, dist, dv, dv_send, dv_recv, dv_half, key_halo, value_send, value_halo,
    whole, ga, gb, ra, rb, ra2, rb2, moments, grads, n_send, n_one, n_two_send, n_two, norms,
    send_sem, recv_sem,
):
    ctx = lax.axis_index("ctx")
    wrk = lax.axis_index("work")
    z, y, x = ctx // (NY * NX), lax.rem(ctx // NX, NY), lax.rem(ctx, NX)
    zh, core = wrk // 2, lax.rem(wrk, 2)
    zx, zy = z * NX + x, z * NY + y
    nxt = lax.rem(ctx + 1, NCTX)
    prv = lax.rem(ctx + NCTX - 1, NCTX)

    def at_ctx(zz, yy, xx):
        return {"ctx": (zz * NY + yy) * NX + xx}

    def zx_peer(k):
        other = lax.rem(zx + k, NZ * NX)
        return other // NX, lax.rem(other, NX)

    def zy_peer(k):
        other = lax.rem(zy + k, NZ * NY)
        return other // NY, lax.rem(other, NY)

    used = [0]
    pending = []

    def send(src, dst, device):
        sem = used[0]
        used[0] += 1
        copy = pltpu.make_async_remote_copy(
            src_ref=src,
            dst_ref=dst,
            send_sem=send_sem.at[sem],
            recv_sem=recv_sem.at[sem],
            device_id=device,
            device_id_type=pl.DeviceIdType.MESH,
        )
        copy.start()
        pending.append(copy)
        return copy

    barrier = pltpu.get_barrier_semaphore()
    greeted = [{"ctx": nxt}, {"ctx": prv}]
    for k in range(1, NZ * NX):
        zz, xx = zx_peer(k)
        greeted.append(at_ctx(zz, y, xx))
    for k in range(1, NZ * NY):
        zz, yy = zy_peer(k)
        greeted.append(at_ctx(zz, yy, x))
    for k in range(1, NW):
        greeted.append({"work": lax.rem(wrk + k, NW)})
    for device in greeted:
        pl.semaphore_signal(barrier, inc=1, device_id=device, device_id_type=pl.DeviceIdType.MESH)

    low_lane = lax.broadcasted_iota(jnp.int32, (1, 128), 1) < HD

    def widen(source, target, first, count):
        for pair in range(KH // 2):
            tile = source[:, pair * 128 : pair * 128 + 128].astype(F32)
            other = pltpu.roll(tile, HD, 1)
            at = pl.ds(first, count)
            target[2 * pair, 0, at, :] = jnp.where(low_lane, tile, 0.0).astype(BF16)
            target[2 * pair, 1, at, :] = jnp.where(low_lane, 0.0, other).astype(BF16)
            target[2 * pair + 1, 0, at, :] = jnp.where(low_lane, other, 0.0).astype(BF16)
            target[2 * pair + 1, 1, at, :] = jnp.where(low_lane, 0.0, tile).astype(BF16)

    spare = jnp.zeros((PAD - OWN, KH * HD), F32)
    for index, source in enumerate((weight, one, two)):
        moments[zh, core, index] = jnp.concatenate([source[...], spare], 0)
    whole[z, y, x] = jnp.concatenate([weight[...], spare], 0).astype(BF16)
    widen(keys[...], k2, SPAN, ROWS)
    for block in range(2):
        apart = (
            lax.broadcasted_iota(jnp.int32, (ROWS, SPAN), 1)
            + SPAN
            - lax.broadcasted_iota(jnp.int32, (ROWS, SPAN), 0)
        )
        near = (apart >= 0) & (apart <= positions[:, block * SPAN : block * SPAN + SPAN])
        dist[block] = jnp.where(near, apart, 1 << 20)

    pl.semaphore_wait(barrier, len(greeted))

    keys_in = send(keys.at[pl.ds(ROWS - SPAN, SPAN)], key_halo, {"ctx": nxt})
    whole_y = [
        send(whole.at[z, y, x], whole.at[z, y, x], at_ctx(z, lax.rem(y + k, NY), x)) for k in range(1, NY)
    ]

    def over_work(buffer):
        far = [
            send(buffer.at[zh, core], buffer.at[zh, core], {"work": lax.rem(zh + k, NH) * 2 + core})
            for k in range(1, NH)
        ]
        near = [send(buffer.at[zh, core], buffer.at[zh, core], {"work": zh * 2 + 1 - core})]

        def forward():
            for k in range(1, NH):
                far[k - 1].wait_recv()
                source = lax.rem(zh + NH - k, NH)
                near.append(
                    send(buffer.at[source, core], buffer.at[source, core], {"work": zh * 2 + 1 - core})
                )

        def arrive():
            for copy in near:
                copy.wait_recv()

        return forward, arrive

    moments_forward, moments_arrive = over_work(moments)

    for tile in range(TILES):
        low, width = window(tile)
        acts_t[tile * 128 : tile * 128 + 128, :] = lax.dot_general(
            spread[tile, :, :width],
            acts[:, low : low + width],
            (((1,), (1,)), ((), ())),
            preferred_element_type=F32,
        ).astype(BF16)

    factor = HD**-0.5 * math.log2(math.e)

    def attend(pair, block):
        rows = slice(block * SPAN, block * SPAN + SPAN)
        span = slice(block * SPAN, block * SPAN + ROWS)

        def head(index, carry):
            j = 2 * pair + index
            first = pl.multiple_of(j * 512, 512)
            for i in range(4):
                query = queries[rows, pl.ds(pl.multiple_of(first + i * 128, 128), 128)]
                for e in range(2):
                    scores = lax.dot_general(
                        k2[j, e, span, :], query, (((1,), (1,)), ((), ())), preferred_element_type=F32
                    )
                    scores = jnp.where(dist[block] <= bands[j * 8 + 2 * i + e], scores, -1e30)
                    top = jnp.max(scores, axis=0, keepdims=True)
                    expo = jnp.exp2((scores - top) * factor)
                    total = jnp.sum(expo, axis=0, keepdims=True)
                    probs[block, j, e, :, i * 128 : i * 128 + 128] = (expo * (1.0 / total)).astype(BF16)
            cotan = jnp.concatenate(
                [out_grad[rows, pl.ds(pl.multiple_of(first + i * 128, 128), 128)] for i in range(4)], 0
            )
            even = jnp.dot(probs[block, j, 0], cotan, preferred_element_type=F32)
            odd = jnp.dot(probs[block, j, 1], cotan, preferred_element_type=F32)
            dv[block, j] = even + pltpu.roll(odd, HD, 1)
            return carry

        lax.fori_loop(0, 2, head, 0)

    def joined(pair, block):
        return jnp.where(low_lane, dv[block, 2 * pair], pltpu.roll(dv[block, 2 * pair + 1], HD, 1))

    def halo_back(pair):
        dv_send[pair] = joined(pair, 0)[:SPAN]
        return send(dv_send.at[pair], dv_recv.at[pair], {"ctx": prv})

    def value_grad(pair, halo):
        first, second = joined(pair, 0), joined(pair, 1)
        halo.wait_recv()
        dv_half[pair, :SPAN, :] = (first[SPAN:] + second[:SPAN]).astype(BF16)
        dv_half[pair, SPAN:, :] = (second[SPAN:] + dv_recv[pair]).astype(BF16)

    attend(0, 1)
    keys_in.wait_recv()
    widen(key_halo[...], k2, 0, SPAN)
    attend(0, 0)
    halo_a = halo_back(0)
    for copy in whole_y:
        copy.wait_recv()
    whole_x = [
        send(whole.at[z, :, x], whole.at[z, :, x], at_ctx(z, y, lax.rem(x + k, NX))) for k in range(1, NX)
    ]
    attend(1, 1)
    value_grad(0, halo_a)

    def grad_a(i, carry):
        rows = pl.ds(pl.multiple_of(i * 768, 768), 768)
        ga[pl.ds(i * 4, 4)] = jnp.dot(acts_t[rows, :], dv_half[0], preferred_element_type=F32).reshape(
            4, NX, PAD, 128
        )
        return carry

    lax.fori_loop(0, 4, grad_a, 0)
    ring_a = Ring(
        NY, y, lambda t, h: ga.at[h * NY + t], ra, send_sem, recv_sem, 100,
        lambda way: at_ctx(z, lax.rem(y + way + NY, NY), x),
    )
    ring_a.step(0)
    attend(1, 0)
    halo_b = halo_back(1)
    moments_forward()
    ring_a.step(1)
    for copy in whole_x:
        copy.wait_recv()
    whole_z = send(whole.at[z], whole.at[z], at_ctx(1 - z, y, x))
    value_grad(1, halo_b)

    def grad_b(i, carry):
        for h in range(NZ):
            rows = pl.ds(pl.multiple_of(h * 1536 + i * 384, 384), 384)
            block = jnp.dot(acts_t[rows, :], dv_half[1], preferred_element_type=F32).reshape(
                2, NX, PAD, 128
            )
            for t in range(NX):
                gb[h, t, pl.ds(i * 2, 2)] = block[:, t]
        return carry

    lax.fori_loop(0, 4, grad_b, 0)
    ring_b = Ring(
        NX, x, lambda t, h: gb.at[h, t], rb, send_sem, recv_sem, 114,
        lambda way: at_ctx(z, y, lax.rem(x + way + NX, NX)),
    )
    ring_b.step(0)
    ring_a.step(2)
    ring_b.step(1)
    for tile in range(TILES):
        low, width = window(tile)
        acts_pad[:, tile * 128 : tile * 128 + 128] = lax.dot_general(
            acts[:, low : low + width],
            spread[tile, :, :width],
            (((1,), (1,)), ((), ())),
            preferred_element_type=F32,
        ).astype(BF16)
    ring_a.step(3)
    ring_b.step(2)
    ring_a.step(4)

    second_a = []
    for k in range(1, NZ * NX):
        zz, xx = zx_peer(k)
        second_a.append(send(ga.at[zz * NY + y, xx], ra2.at[k - 1], at_ctx(zz, y, xx)))
    second_b = []
    for k in range(1, NZ * NY):
        zz, yy = zy_peer(k)
        second_b.append(send(gb.at[zz, x, yy], rb2.at[k - 1], at_ctx(zz, yy, x)))

    whole_z.wait_recv()
    values = jnp.dot(
        acts_pad[...], whole[...].reshape(NCTX * PAD, KH * HD), preferred_element_type=F32
    ).astype(BF16)
    value_send[...] = values[ROWS - SPAN :]
    values_in = send(value_send, value_halo, {"ctx": nxt})
    widen(values, v2, SPAN, ROWS)

    def output(block):
        rows = slice(block * SPAN, block * SPAN + SPAN)
        span = slice(block * SPAN, block * SPAN + ROWS)

        def head(j, carry):
            total = jnp.zeros((512, 128), F32)
            for e in range(2):
                total += lax.dot_general(
                    probs[block, j, e], v2[j, e, span, :], (((0,), (0,)), ((), ())), preferred_element_type=F32
                )
            for i in range(4):
                out[rows, pl.ds(pl.multiple_of(j * 512 + i * 128, 128), 128)] = total[
                    i * 128 : i * 128 + 128
                ].astype(BF16)
            return carry

        lax.fori_loop(0, KH, head, 0)

    output(1)
    for copy in second_a:
        copy.wait_recv()
    half_a = ga[z * NY + y, x]
    for k in range(1, NZ * NX):
        half_a = half_a + ra2[k - 1]
    for copy in second_b:
        copy.wait_recv()
    half_b = gb[z, x, y]
    for k in range(1, NZ * NY):
        half_b = half_b + rb2[k - 1]
    tokens_all = float(ROWS * NCTX)
    half_a, half_b = half_a / tokens_all, half_b / tokens_all
    grads[zh, core, :, :128] = half_a
    grads[zh, core, :, 128:] = half_b
    grads_forward, grads_arrive = over_work(grads)
    n_send[...] = (half_a * half_a + half_b * half_b).reshape(PAD // 8, 8, 128).sum(0)
    norm_one = []
    for k in range(1, NZ * NX):
        zz, xx = zx_peer(k)
        norm_one.append(send(n_send, n_one.at[k - 1], at_ctx(zz, y, xx)))
    values_in.wait_recv()
    widen(value_halo[...], v2, 0, SPAN)
    for copy in norm_one:
        copy.wait_recv()
    n_two_send[...] = n_send[...] + n_one[...].sum(0)
    norm_two = [
        send(n_two_send, n_two.at[k - 1], at_ctx(z, lax.rem(y + k, NY), x)) for k in range(1, NY)
    ]
    grads_forward()
    for copy in norm_two:
        copy.wait_recv()
    norms[wrk] = n_two_send[...] + n_two[...].sum(0)
    norm_work = [
        send(norms.at[wrk], norms.at[wrk], {"work": lax.rem(wrk + k, NW)}) for k in range(1, NW)
    ]
    output(0)
    moments_arrive()
    grads_arrive()
    for copy in norm_work:
        copy.wait_recv()

    count = jnp.full((1, 128), step[0].astype(F32), F32)
    fix_one = (1.0 - jnp.exp(count * math.log(beta_one)))[:, :1]
    fix_two = (1.0 - jnp.exp(count * math.log(beta_two)))[:, :1]
    sums = [jnp.zeros((PAD, KH * HD), F32) for _ in range(3)]
    for w in range(NW):
        square = jnp.sum(jnp.sum(norms[w], axis=0, keepdims=True), axis=1, keepdims=True)
        scale = jnp.minimum(1.0, clip_norm / (jnp.sqrt(square) + 1e-06))
        grad = grads[w // 2, w % 2] * scale
        first = beta_one * moments[w // 2, w % 2, 1] + (1.0 - beta_one) * grad
        second = beta_two * moments[w // 2, w % 2, 2] + (1.0 - beta_two) * grad * grad
        updated = moments[w // 2, w % 2, 0] - learn_rate * (first / fix_one) / (
            jnp.sqrt(second / fix_two) + adam_eps
        )
        sums = [total + part for total, part in zip(sums, (updated, first, second))]
    for target, total in zip((mean_weight, mean_one, mean_two), sums):
        target[...] = (total / NW)[:OWN]

    for copy in pending:
        copy.wait_send()
    ring_a.finish()
    ring_b.finish()


def per_device(
    inputs, queries, keys, out_grad, positions, bands, step, value_weight, moment_one, moment_two
):
    vmem = pl.BlockSpec(memory_space=pltpu.VMEM)
    smem = pl.BlockSpec(memory_space=pltpu.SMEM)
    width = KH * HD
    out, mean_weight, mean_one, mean_two = pl.pallas_call(
        kernel,
        out_shape=(
            jax.ShapeDtypeStruct((ROWS, QH * HD), BF16),
            *[jax.ShapeDtypeStruct((OWN, width), F32)] * 3,
        ),
        in_specs=[vmem, vmem, vmem, vmem, vmem, smem, smem, vmem, vmem, vmem, vmem],
        out_specs=(vmem, vmem, vmem, vmem),
        scratch_shapes=[
            pltpu.VMEM((ROWS, NCTX * PAD), BF16),
            pltpu.VMEM((NCTX * PAD, ROWS), BF16),
            pltpu.VMEM((KH, 2, SPAN + ROWS, 128), BF16),
            pltpu.VMEM((KH, 2, SPAN + ROWS, 128), BF16),
            pltpu.VMEM((2, KH, 2, ROWS, 512), BF16),
            pltpu.VMEM((2, ROWS, SPAN), jnp.int32),
            pltpu.VMEM((2, KH, ROWS, 128), F32),
            pltpu.VMEM((2, SPAN, 128), F32),
            pltpu.VMEM((2, SPAN, 128), F32),
            pltpu.VMEM((2, ROWS, 128), BF16),
            pltpu.VMEM((SPAN, width), BF16),
            pltpu.VMEM((SPAN, width), BF16),
            pltpu.VMEM((SPAN, width), BF16),
            pltpu.VMEM((NZ, NY, NX, PAD, width), BF16),
            pltpu.VMEM((NZ * NY, NX, PAD, 128), F32),
            pltpu.VMEM((NZ, NX, NY, PAD, 128), F32),
            pltpu.VMEM((14, NX, PAD, 128), F32),
            pltpu.VMEM((6, NY, PAD, 128), F32),
            pltpu.VMEM((NZ * NX - 1, PAD, 128), F32),
            pltpu.VMEM((NZ * NY - 1, PAD, 128), F32),
            pltpu.VMEM((NH, 2, 3, PAD, width), F32),
            pltpu.VMEM((NH, 2, PAD, width), F32),
            pltpu.VMEM((8, 128), F32),
            pltpu.VMEM((NZ * NX - 1, 8, 128), F32),
            pltpu.VMEM((8, 128), F32),
            pltpu.VMEM((NY - 1, 8, 128), F32),
            pltpu.VMEM((NW, 8, 128), F32),
            pltpu.SemaphoreType.DMA((120,)),
            pltpu.SemaphoreType.DMA((120,)),
        ],
        compiler_params=pltpu.CompilerParams(
            collective_id=0, has_side_effects=True, vmem_limit_bytes=48 * 1024 * 1024
        ),
        name="local_adam",
    )(
        inputs[0], queries[0], keys[0], out_grad[0], positions, bands, step,
        value_weight[0], moment_one[0], moment_two[0], jnp.asarray(spread_matrix(), BF16),
    )
    return out[None], mean_weight, mean_one, mean_two


def solution(mesh):
    rows = P("work", "ctx", None)
    in_specs = (rows, rows, rows, rows, P("work", "ctx"), P(), P(), rows, rows, rows)
    out_specs = (rows, P("ctx", None), P("ctx", None), P("ctx", None))
    return jax.shard_map(
        per_device, mesh=mesh, in_specs=in_specs, out_specs=out_specs, check_vma=False
    )
```

time: 264 us -> 93.1 us (0.35); the launches traced: 260 us -> 92.8 us
  blocking collectives: 84.1 us -> 0 us
  Pallas kernels: 0 us -> 83.8 us
  waiting for transfers between devices: 49.7 us -> 0 us
  starting transfers between devices: 36.2 us -> 0 us
  local copies, waits for them, and re-layouts: 38.5 us -> 7.6 us
  matrix products: 30.8 us -> 0 us
  other arithmetic: 18.4 us -> 0 us
    all_to_all x1 -> x0, blocking collectives: 84.1 us -> none  [sent_and_summed(): lax.all_to_all(blocks, axis, split_axis=0, concat_axis=0, tiled=True)]
    pallas_call x0 -> x1, Pallas kernels: none -> 83.8 us  [per_device(): pl.pallas_call(kernel, out_shape=(jax.ShapeDtypeStruct((ROWS, QH * HD), B...]
    all_to_all x3 -> x0, waiting for transfers between devices: 43.8 us -> none  [from_everyone(): return lax.all_to_all(copies, axis, split_axis=0, concat_axis=0, tiled=True)]
    all_to_all x3 -> x0, starting transfers between devices: 28 us -> none  [from_everyone(): return lax.all_to_all(copies, axis, split_axis=0, concat_axis=0, tiled=True)]
    sub x4 -> x0, matrix products: 16.2 us -> none  [attend(): expo = jnp.exp(scores - top)]
    dot_general x10 -> x0, matrix products: 14.6 us -> none  [the longest x4 7.42 us: attend(): jnp.einsum('gqk,kd->qgd', probs, valued, preferred_element_type=jnp.float32)]
    slice x15 -> x0, local copies, waits for them, and re-layouts: 14.4 us -> none  [the longest x5 7.68 us: attend(): query = qrows[:, lo:hi].reshape(count, group, HD)]
    convert_element_type x4 -> x0, other arithmetic: 8.77 us -> none  [attend(): probs = (expo / jnp.sum(expo, axis=2, keepdims=True)).astype(jnp.bfloat16)]
  transfers between devices with their start and end apart: 6 -> 0, of which waited for: 5 -> 0; matrix products, arithmetic and copies ran while one was open for 14% -> 0% of each run, Pallas kernels for 0% -> 0%
where the time goes in v1:
time: 93.1 us; the launch traced here: 92.8 us
  Pallas kernels  83.8 us (90%)
  local copies, waits for them, and re-layouts  7.6 us (8%)
  between operations  1.37 us (1%)
    pallas_call x1, Pallas kernels, per_device(): pl.pallas_call(kernel, out_shape=(jax.ShapeDtypeStruct((ROWS, QH * HD), B...  83.8 us
    unnamed x17, local copies, waits for them, and re-layouts  7.6 us

profile of v1, /device:TPU:1, one launch (start us, length us, event | category | flops | bytes accessed | tf_op | source)
XLA Modules:
  0.0 92.8 jit_solution(2961609297377234398)
XLA Ops:
  1.3 0.8 copy.22
  2.1 0.8 copy_bitcast_fusion
  2.9 0.0 copy-start
  2.9 0.0 copy-start.2
  2.9 0.0 copy-start.3
  2.9 0.0 copy-start.4
  2.9 1.9 %copy.15 = bf16[1,256,2880]{2,1,0:T(8,128)(2,1)S(1)} copy(bf16[1,256,2880]{1,2,0:T(8,128)(2,1)} %param.11) | data formatting | bytes 2949120 | tf_op args[0]
  4.9 0.0 copy-done
  4.9 0.0 copy-done.2
  4.9 0.0 copy-done.3
  4.9 0.0 copy-done.4
  4.9 0.0 copy-start.1
  4.9 1.2 %copy-done.1 = bf16[1,256,2048]{2,1,0:T(8,128)(2,1)S(1)} copy-done((bf16[1,256,2048]{2,1,0:T(8,128)(2,1)S(1)}, bf16[1,256,2048]{2,1,0:T(8,128)(2,1)}, u32[]{:S(2)}) %copy-start.1) | copy-done | bytes 1048600
  6.1 83.8 %local_adam.1 = (bf16[256,2048]{1,0:T(8,128)(2,1)S(1)}, f32[45,256]{1,0:T(8,128)S(1)}, f32[45,256]{1,0:T(8,128)S(1)}, f32[45,256]{1,0:T(8,128)S(1)}) custom-call(bf16[256,2880]{1,0:T(8,128)(2,1)S(1)} %bitcast.12, bf16[256,2048]{1,0:T(8,128)(2,1)S(1)} %bitcast.13, bf16[256,256]{1,0:T(8,128)(2,1)S(1)} %bitcast.17, bf16[256,2048]{1,0:T(8,128)(2,1)S(1)} %bitcast.14, ...), custom_call_target="tpu_custom_call" | custom-call | tf_op jit(solution)/shard_map/local_adam/pallas_call | solution.py:444
  90.0 1.0 %copy.28 = bf16[1,256,2048]{2,1,0:T(8,128)(2,1)} copy(bf16[1,256,2048]{2,1,0:T(8,128)(2,1)S(1)} %bitcast.15) | data formatting | bytes 2097152
  90.9 0.6 copy.29
  91.5 0.6 copy.30
  92.2 0.6 copy.31
Async XLA Ops:
  2.9 2.0 %copy-start = (bf16[1,256,2048]{2,1,0:T(8,128)(2,1)S(1)}, bf16[1,256,2048]{2,1,0:T(8,128)(2,1)}, u32[]{:S(2)}) copy-start(bf16[1,256,2048]{2,1,0:T(8,128)(2,1)} %param.12) | copy-start | bytes 3145732
  2.9 2.0 %copy-start.2 = (bf16[1,256,256]{2,1,0:T(8,128)(2,1)S(1)}, bf16[1,256,256]{2,1,0:T(8,128)(2,1)}, u32[]{:S(2)}) copy-start(bf16[1,256,256]{2,1,0:T(8,128)(2,1)} %param.13) | copy-start | bytes 393220
  2.9 2.0 %copy-start.3 = (s32[1,256]{1,0:T(1,128)S(1)}, s32[1,256]{1,0:T(1,128)}, u32[]{:S(2)}) copy-start(s32[1,256]{1,0:T(1,128)} %positions.1) | copy-start | bytes 3076
  2.9 2.0 %copy-start.4 = (s32[32]{0:T(128)S(1)}, s32[32]{0:T(128)}, u32[]{:S(2)}) copy-start(s32[32]{0:T(128)} %bands.1) | copy-start | bytes 388
  4.9 1.2 %copy-start.1 = (bf16[1,256,2048]{2,1,0:T(8,128)(2,1)S(1)}, bf16[1,256,2048]{2,1,0:T(8,128)(2,1)}, u32[]{:S(2)}) copy-start(bf16[1,256,2048]{2,1,0:T(8,128)(2,1)} %param.14) | copy-start | bytes 3145732

commit v2 on v1

--- a/solution.py
+++ b/solution.py
@@ -106,11 +106,11 @@
 
 
 def kernel(
-    acts, queries, keys, out_grad, positions, bands, step, weight, one, two, spread,
-    out, mean_weight, mean_one, mean_two,
-    acts_pad, acts_t, k2, v2, probs, dist, dv, dv_send, dv_recv, dv_half, key_halo, value_send, value_halo,
+    acts_hbm, queries_hbm, keys_hbm, out_grad_hbm, positions_hbm, bands, step, weight_hbm, one_hbm, two_hbm, spread_hbm,
+    out_hbm, mean_weight, mean_one, mean_two,
+    out, acts, queries, keys, out_grad, positions, state, spread, acts_t, k2, v2, probs, dist, dv, dv_send, dv_recv, dv_half, key_halo, value_send, value_halo,
     whole, ga, gb, ra, rb, ra2, rb2, moments, grads, n_send, n_one, n_two_send, n_two, norms,
-    send_sem, recv_sem,
+    send_sem, recv_sem, load_sem,
 ):
     ctx = lax.axis_index("ctx")
     wrk = lax.axis_index("work")
@@ -149,6 +149,16 @@
         pending.append(copy)
         return copy
 
+    loads = []
+    for index, (source, target) in enumerate((
+        (keys_hbm, keys), (positions_hbm, positions), (queries_hbm, queries), (out_grad_hbm, out_grad),
+        (weight_hbm, state.at[0]), (one_hbm, state.at[1]), (two_hbm, state.at[2]),
+        (spread_hbm, spread), (acts_hbm, acts),
+    )):
+        load = pltpu.make_async_copy(source, target, load_sem.at[index])
+        load.start()
+        loads.append(load)
+
     barrier = pltpu.get_barrier_semaphore()
     greeted = [{"ctx": nxt}, {"ctx": prv}]
     for k in range(1, NZ * NX):
@@ -174,10 +184,8 @@
             target[2 * pair + 1, 0, at, :] = jnp.where(low_lane, other, 0.0).astype(BF16)
             target[2 * pair + 1, 1, at, :] = jnp.where(low_lane, 0.0, tile).astype(BF16)
 
-    spare = jnp.zeros((PAD - OWN, KH * HD), F32)
-    for index, source in enumerate((weight, one, two)):
-        moments[zh, core, index] = jnp.concatenate([source[...], spare], 0)
-    whole[z, y, x] = jnp.concatenate([weight[...], spare], 0).astype(BF16)
+    for load in loads[:2]:
+        load.wait()
     widen(keys[...], k2, SPAN, ROWS)
     for block in range(2):
         apart = (
@@ -187,45 +195,6 @@
         )
         near = (apart >= 0) & (apart <= positions[:, block * SPAN : block * SPAN + SPAN])
         dist[block] = jnp.where(near, apart, 1 << 20)
-
-    pl.semaphore_wait(barrier, len(greeted))
-
-    keys_in = send(keys.at[pl.ds(ROWS - SPAN, SPAN)], key_halo, {"ctx": nxt})
-    whole_y = [
-        send(whole.at[z, y, x], whole.at[z, y, x], at_ctx(z, lax.rem(y + k, NY), x)) for k in range(1, NY)
-    ]
-
-    def over_work(buffer):
-        far = [
-            send(buffer.at[zh, core], buffer.at[zh, core], {"work": lax.rem(zh + k, NH) * 2 + core})
-            for k in range(1, NH)
-        ]
-        near = [send(buffer.at[zh, core], buffer.at[zh, core], {"work": zh * 2 + 1 - core})]
-
-        def forward():
-            for k in range(1, NH):
-                far[k - 1].wait_recv()
-                source = lax.rem(zh + NH - k, NH)
-                near.append(
-                    send(buffer.at[source, core], buffer.at[source, core], {"work": zh * 2 + 1 - core})
-                )
-
-        def arrive():
-            for copy in near:
-                copy.wait_recv()
-
-        return forward, arrive
-
-    moments_forward, moments_arrive = over_work(moments)
-
-    for tile in range(TILES):
-        low, width = window(tile)
-        acts_t[tile * 128 : tile * 128 + 128, :] = lax.dot_general(
-            spread[tile, :, :width],
-            acts[:, low : low + width],
-            (((1,), (1,)), ((), ())),
-            preferred_element_type=F32,
-        ).astype(BF16)
 
     factor = HD**-0.5 * math.log2(math.e)
 
@@ -270,17 +239,65 @@
         dv_half[pair, :SPAN, :] = (first[SPAN:] + second[:SPAN]).astype(BF16)
         dv_half[pair, SPAN:, :] = (second[SPAN:] + dv_recv[pair]).astype(BF16)
 
+    for load in loads[2:4]:
+        load.wait()
     attend(0, 1)
+    for load in loads[4:7]:
+        load.wait()
+    spare = jnp.zeros((PAD - OWN, KH * HD), F32)
+    for index in range(3):
+        moments[zh, core, index] = jnp.concatenate([state[index, :, 0, :], spare], 0)
+    whole[z, y, x] = moments[zh, core, 0].astype(BF16)
+
+    pl.semaphore_wait(barrier, len(greeted))
+
+    keys_in = send(keys.at[pl.ds(ROWS - SPAN, SPAN)], key_halo, {"ctx": nxt})
+    whole_y = [
+        send(whole.at[z, y, x], whole.at[z, y, x], at_ctx(z, lax.rem(y + k, NY), x)) for k in range(1, NY)
+    ]
+
+    def over_work(buffer):
+        far = [
+            send(buffer.at[zh, core], buffer.at[zh, core], {"work": lax.rem(zh + k, NH) * 2 + core})
+            for k in range(1, NH)
+        ]
+        near = [send(buffer.at[zh, core], buffer.at[zh, core], {"work": zh * 2 + 1 - core})]
+
+        def forward():
+            for k in range(1, NH):
+                far[k - 1].wait_recv()
+                source = lax.rem(zh + NH - k, NH)
+                near.append(
+                    send(buffer.at[source, core], buffer.at[source, core], {"work": zh * 2 + 1 - core})
+                )
+
+        def arrive():
+            for copy in near:
+                copy.wait_recv()
+
+        return forward, arrive
+
+    moments_forward, moments_arrive = over_work(moments)
+
+    for load in loads[7:]:
+        load.wait()
+    for tile in range(TILES):
+        low, width = window(tile)
+        acts_t[tile * 128 : tile * 128 + 128, :] = jnp.dot(
+            spread[tile, :, :width], acts[low : low + width, :], preferred_element_type=F32
+        ).astype(BF16)
+    attend(1, 1)
     keys_in.wait_recv()
     widen(key_halo[...], k2, 0, SPAN)
     attend(0, 0)
     halo_a = halo_back(0)
+    attend(1, 0)
+    halo_b = halo_back(1)
     for copy in whole_y:
         copy.wait_recv()
     whole_x = [
         send(whole.at[z, :, x], whole.at[z, :, x], at_ctx(z, y, lax.rem(x + k, NX))) for k in range(1, NX)
     ]
-    attend(1, 1)
     value_grad(0, halo_a)
 
     def grad_a(i, carry):
@@ -296,13 +313,6 @@
         lambda way: at_ctx(z, lax.rem(y + way + NY, NY), x),
     )
     ring_a.step(0)
-    attend(1, 0)
-    halo_b = halo_back(1)
-    moments_forward()
-    ring_a.step(1)
-    for copy in whole_x:
-        copy.wait_recv()
-    whole_z = send(whole.at[z], whole.at[z], at_ctx(1 - z, y, x))
     value_grad(1, halo_b)
 
     def grad_b(i, carry):
@@ -321,16 +331,13 @@
         lambda way: at_ctx(z, y, lax.rem(x + way + NX, NX)),
     )
     ring_b.step(0)
+    moments_forward()
+    ring_a.step(1)
+    for copy in whole_x:
+        copy.wait_recv()
+    whole_z = send(whole.at[z], whole.at[z], at_ctx(1 - z, y, x))
     ring_a.step(2)
     ring_b.step(1)
-    for tile in range(TILES):
-        low, width = window(tile)
-        acts_pad[:, tile * 128 : tile * 128 + 128] = lax.dot_general(
-            acts[:, low : low + width],
-            spread[tile, :, :width],
-            (((1,), (1,)), ((), ())),
-            preferred_element_type=F32,
-        ).astype(BF16)
     ring_a.step(3)
     ring_b.step(2)
     ring_a.step(4)
@@ -345,8 +352,8 @@
         second_b.append(send(gb.at[zz, x, yy], rb2.at[k - 1], at_ctx(zz, yy, x)))
 
     whole_z.wait_recv()
-    values = jnp.dot(
-        acts_pad[...], whole[...].reshape(NCTX * PAD, KH * HD), preferred_element_type=F32
+    values = lax.dot_general(
+        acts_t[...], whole[...].reshape(NCTX * PAD, KH * HD), (((0,), (0,)), ((), ())), preferred_element_type=F32
     ).astype(BF16)
     value_send[...] = values[ROWS - SPAN :]
     values_in = send(value_send, value_halo, {"ctx": nxt})
@@ -370,7 +377,6 @@
 
         lax.fori_loop(0, KH, head, 0)
 
-    output(1)
     for copy in second_a:
         copy.wait_recv()
     half_a = ga[z * NY + y, x]
@@ -391,6 +397,7 @@
     for k in range(1, NZ * NX):
         zz, xx = zx_peer(k)
         norm_one.append(send(n_send, n_one.at[k - 1], at_ctx(zz, y, xx)))
+    output(1)
     values_in.wait_recv()
     widen(value_halo[...], v2, 0, SPAN)
     for copy in norm_one:
@@ -400,13 +407,15 @@
         send(n_two_send, n_two.at[k - 1], at_ctx(z, lax.rem(y + k, NY), x)) for k in range(1, NY)
     ]
     grads_forward()
+    output(0)
+    store = pltpu.make_async_copy(out, out_hbm, load_sem.at[9])
+    store.start()
     for copy in norm_two:
         copy.wait_recv()
     norms[wrk] = n_two_send[...] + n_two[...].sum(0)
     norm_work = [
         send(norms.at[wrk], norms.at[wrk], {"work": lax.rem(wrk + k, NW)}) for k in range(1, NW)
     ]
-    output(0)
     moments_arrive()
     grads_arrive()
     for copy in norm_work:
@@ -429,16 +438,27 @@
     for target, total in zip((mean_weight, mean_one, mean_two), sums):
         target[...] = (total / NW)[:OWN]
 
+    store.wait()
     for copy in pending:
         copy.wait_send()
     ring_a.finish()
     ring_b.finish()
 
 
+def hand_over(*refs):
+    sems = refs[-1]
+    copies = [pltpu.make_async_copy(refs[i], refs[4 + i], sems.at[i]) for i in range(4)]
+    for copy in copies:
+        copy.start()
+    for copy in copies:
+        copy.wait()
+
+
 def per_device(
     inputs, queries, keys, out_grad, positions, bands, step, value_weight, moment_one, moment_two
 ):
     vmem = pl.BlockSpec(memory_space=pltpu.VMEM)
+    hbm = pl.BlockSpec(memory_space=pltpu.HBM)
     smem = pl.BlockSpec(memory_space=pltpu.SMEM)
     width = KH * HD
     out, mean_weight, mean_one, mean_two = pl.pallas_call(
@@ -447,10 +467,17 @@
             jax.ShapeDtypeStruct((ROWS, QH * HD), BF16),
             *[jax.ShapeDtypeStruct((OWN, width), F32)] * 3,
         ),
-        in_specs=[vmem, vmem, vmem, vmem, vmem, smem, smem, vmem, vmem, vmem, vmem],
-        out_specs=(vmem, vmem, vmem, vmem),
+        in_specs=[hbm, hbm, hbm, hbm, hbm, smem, smem, hbm, hbm, hbm, hbm],
+        out_specs=(hbm, vmem, vmem, vmem),
         scratch_shapes=[
-            pltpu.VMEM((ROWS, NCTX * PAD), BF16),
+            pltpu.VMEM((ROWS, QH * HD), BF16),
+            pltpu.VMEM((D, ROWS), BF16),
+            pltpu.VMEM((ROWS, QH * HD), BF16),
+            pltpu.VMEM((ROWS, width), BF16),
+            pltpu.VMEM((ROWS, QH * HD), BF16),
+            pltpu.VMEM((1, ROWS), jnp.int32),
+            pltpu.VMEM((3, OWN, 1, width), F32),
+            pltpu.VMEM((TILES, 128, 256), BF16),
             pltpu.VMEM((NCTX * PAD, ROWS), BF16),
             pltpu.VMEM((KH, 2, SPAN + ROWS, 128), BF16),
             pltpu.VMEM((KH, 2, SPAN + ROWS, 128), BF16),
@@ -479,15 +506,25 @@
             pltpu.VMEM((NW, 8, 128), F32),
             pltpu.SemaphoreType.DMA((120,)),
             pltpu.SemaphoreType.DMA((120,)),
+            pltpu.SemaphoreType.DMA((10,)),
         ],
         compiler_params=pltpu.CompilerParams(
-            collective_id=0, has_side_effects=True, vmem_limit_bytes=48 * 1024 * 1024
+            collective_id=0, has_side_effects=True, vmem_limit_bytes=63 * 1024 * 1024
         ),
         name="local_adam",
     )(
-        inputs[0], queries[0], keys[0], out_grad[0], positions, bands, step,
-        value_weight[0], moment_one[0], moment_two[0], jnp.asarray(spread_matrix(), BF16),
+        jnp.swapaxes(inputs[0], 0, 1), queries[0], keys[0], out_grad[0], positions, bands, step,
+        *[jnp.swapaxes(a, 0, 1) for a in (value_weight, moment_one, moment_two)], jnp.asarray(spread_matrix(), BF16),
     )
+    results = (out, mean_weight, mean_one, mean_two)
+    out, mean_weight, mean_one, mean_two = pl.pallas_call(
+        hand_over,
+        out_shape=tuple(jax.ShapeDtypeStruct(a.shape, a.dtype) for a in results),
+        in_specs=[vmem] * 4,
+        out_specs=(hbm,) * 4,
+        scratch_shapes=[pltpu.SemaphoreType.DMA((4,))],
+        name="hand_over",
+    )(*results)
     return out[None], mean_weight, mean_one, mean_two
 
 

time: 93.1 us -> 83.8 us (0.900)
  local copies, waits for them, and re-layouts: 7.6 us -> 0 us
  Pallas kernels: 83.8 us -> 82.4 us
    unnamed x17 -> x0, local copies, waits for them, and re-layouts: 7.6 us -> none
    pallas_call x1, Pallas kernels: 83.8 us -> 80.1 us  [per_device(): pl.pallas_call(kernel, out_shape=(jax.ShapeDtypeStruct((ROWS, QH * HD), B...]
    pallas_call x0 -> x1, Pallas kernels: none -> 2.29 us  [per_device(): pl.pallas_call(hand_over, out_shape=tuple((jax.ShapeDtypeStruct(a.shape,...]
where the time goes in v2:
time: 83.8 us; the launch traced here: 83.7 us
  Pallas kernels  82.4 us (98%)
  between operations  1.29 us (2%)
    pallas_call x1, Pallas kernels, per_device(): pl.pallas_call(kernel, out_shape=(jax.ShapeDtypeStruct((ROWS, QH * HD), B...  80.1 us
    pallas_call x1, Pallas kernels, per_device(): pl.pallas_call(hand_over, out_shape=tuple((jax.ShapeDtypeStruct(a.shape,...  2.29 us

profile of v2, /device:TPU:1, one launch (start us, length us, event | category | flops | bytes accessed | tf_op | source)
XLA Modules:
  0.0 83.7 jit_solution(8893468866963366178)
XLA Ops:
  1.3 80.1 %local_adam.1 = (bf16[256,2048]{1,0:T(8,128)(2,1)}, f32[45,256]{1,0:T(8,128)}, f32[45,256]{1,0:T(8,128)}, f32[45,256]{1,0:T(8,128)}) custom-call(bf16[2880,256]{1,0:T(8,128)(2,1)} %bitcast.10, bf16[256,2048]{1,0:T(8,128)(2,1)} %bitcast.11, bf16[256,256]{1,0:T(8,128)(2,1)} %bitcast.13, bf16[256,2048]{1,0:T(8,128)(2,1)} %bitcast.12, s32[1,256]{1,0:T(1,128)} %positions_hbm.1, ...), custom_call_target="tpu_custom_call" | custom-call | tf_op jit(solution)/shard_map/local_adam/pallas_call | solution.py:464
  81.4 2.3 %hand_over.1 = (bf16[256,2048]{1,0:T(8,128)(2,1)}, f32[45,256]{1,0:T(8,128)}, f32[45,256]{1,0:T(8,128)}, f32[45,256]{1,0:T(8,128)}) custom-call(bf16[256,2048]{1,0:T(8,128)(2,1)} %get-tuple-element.12.refs_0_, f32[45,256]{1,0:T(8,128)} %get-tuple-element.13.refs_1_, f32[45,256]{1,0:T(8,128)} %get-tuple-element.14.refs_2_, f32[45,256]{1,0:T(8,128)} %get-tuple-element.15.refs_3_), custom_call_target="tpu_custom_call" | custom-call | tf_op jit(solution)/shard_map/hand_over/pallas_call | solution.py:520

commit v3 on v2

--- a/solution.py
+++ b/solution.py
@@ -21,7 +21,9 @@
 NW = 8
 OWN = D // NCTX
 PAD = 48
-TILES = NCTX * PAD // 128
+HALF = D // NZ
+HALF_PAD = NY * NX * PAD
+TILES = HALF_PAD // 128
 
 beta_one = 0.9
 beta_two = 0.95
@@ -37,7 +39,7 @@
     lane = tile * 128
     source = OWN * (lane // PAD) + min(lane % PAD, OWN - 1)
     low = source // 128 * 128
-    return low, min(256, D - low)
+    return low, min(256, HALF - low)
 
 
 def spread_matrix():
@@ -109,14 +111,14 @@
     acts_hbm, queries_hbm, keys_hbm, out_grad_hbm, positions_hbm, bands, step, weight_hbm, one_hbm, two_hbm, spread_hbm,
     out_hbm, mean_weight, mean_one, mean_two,
     out, acts, queries, keys, out_grad, positions, state, spread, acts_t, k2, v2, probs, dist, dv, dv_send, dv_recv, dv_half, key_halo, value_send, value_halo,
-    whole, ga, gb, ra, rb, ra2, rb2, moments, grads, n_send, n_one, n_two_send, n_two, norms,
+    other_acts, dv_all, part, part_in, whole, gx, gy, rx, ry, rx2, ry2, moments, grads, n_send, n_one, n_two_send, n_two, norms,
     send_sem, recv_sem, load_sem,
 ):
     ctx = lax.axis_index("ctx")
     wrk = lax.axis_index("work")
     z, y, x = ctx // (NY * NX), lax.rem(ctx // NX, NY), lax.rem(ctx, NX)
     zh, core = wrk // 2, lax.rem(wrk, 2)
-    zx, zy = z * NX + x, z * NY + y
+    zx = z * NX + x
     nxt = lax.rem(ctx + 1, NCTX)
     prv = lax.rem(ctx + NCTX - 1, NCTX)
 
@@ -126,10 +128,6 @@
     def zx_peer(k):
         other = lax.rem(zx + k, NZ * NX)
         return other // NX, lax.rem(other, NX)
-
-    def zy_peer(k):
-        other = lax.rem(zy + k, NZ * NY)
-        return other // NY, lax.rem(other, NY)
 
     used = [0]
     pending = []
@@ -164,9 +162,8 @@
     for k in range(1, NZ * NX):
         zz, xx = zx_peer(k)
         greeted.append(at_ctx(zz, y, xx))
-    for k in range(1, NZ * NY):
-        zz, yy = zy_peer(k)
-        greeted.append(at_ctx(zz, yy, x))
+    for k in range(1, NY):
+        greeted.append(at_ctx(z, lax.rem(y + k, NY), x))
     for k in range(1, NW):
         greeted.append({"work": lax.rem(wrk + k, NW)})
     for device in greeted:
@@ -247,14 +244,14 @@
     spare = jnp.zeros((PAD - OWN, KH * HD), F32)
     for index in range(3):
         moments[zh, core, index] = jnp.concatenate([state[index, :, 0, :], spare], 0)
-    whole[z, y, x] = moments[zh, core, 0].astype(BF16)
+    whole[y, x] = moments[zh, core, 0].astype(BF16)
 
     pl.semaphore_wait(barrier, len(greeted))
 
     keys_in = send(keys.at[pl.ds(ROWS - SPAN, SPAN)], key_halo, {"ctx": nxt})
-    whole_y = [
-        send(whole.at[z, y, x], whole.at[z, y, x], at_ctx(z, lax.rem(y + k, NY), x)) for k in range(1, NY)
-    ]
+    loads[8].wait()
+    acts_in = send(acts.at[1 - z], other_acts, at_ctx(1 - z, y, x))
+    whole_y = [send(whole.at[y, x], whole.at[y, x], at_ctx(z, lax.rem(y + k, NY), x)) for k in range(1, NY)]
 
     def over_work(buffer):
         far = [
@@ -277,15 +274,19 @@
 
         return forward, arrive
 
-    moments_forward, moments_arrive = over_work(moments)
-
-    for load in loads[7:]:
-        load.wait()
-    for tile in range(TILES):
-        low, width = window(tile)
-        acts_t[tile * 128 : tile * 128 + 128, :] = jnp.dot(
-            spread[tile, :, :width], acts[low : low + width, :], preferred_element_type=F32
-        ).astype(BF16)
+    loads[7].wait()
+
+    def spread_out(source, owner):
+        def tile_step(low, width, tile):
+            at = pl.ds(pl.multiple_of(owner * ROWS, ROWS), ROWS)
+            acts_t[tile * 128 : tile * 128 + 128, at] = jnp.dot(
+                spread[tile, :, :width], source[low : low + width, :], preferred_element_type=F32
+            ).astype(BF16)
+
+        for tile in range(TILES):
+            tile_step(*window(tile), tile)
+
+    spread_out(acts.at[z], z)
     attend(1, 1)
     keys_in.wait_recv()
     widen(key_halo[...], k2, 0, SPAN)
@@ -295,66 +296,78 @@
     halo_b = halo_back(1)
     for copy in whole_y:
         copy.wait_recv()
-    whole_x = [
-        send(whole.at[z, :, x], whole.at[z, :, x], at_ctx(z, y, lax.rem(x + k, NX))) for k in range(1, NX)
-    ]
+    mine_x = whole.at[:, x]
+    whole_x = [send(mine_x, mine_x, at_ctx(z, y, lax.rem(x + k, NX))) for k in range(1, NX)]
+
+    def share(pair):
+        at = pl.ds(pl.multiple_of(z * ROWS, ROWS), ROWS)
+        dv_all[pair, at, :] = dv_half[pair]
+        return send(dv_all.at[pair, at], dv_all.at[pair, at], at_ctx(1 - z, y, x))
+
     value_grad(0, halo_a)
-
-    def grad_a(i, carry):
-        rows = pl.ds(pl.multiple_of(i * 768, 768), 768)
-        ga[pl.ds(i * 4, 4)] = jnp.dot(acts_t[rows, :], dv_half[0], preferred_element_type=F32).reshape(
-            4, NX, PAD, 128
-        )
-        return carry
-
-    lax.fori_loop(0, 4, grad_a, 0)
-    ring_a = Ring(
-        NY, y, lambda t, h: ga.at[h * NY + t], ra, send_sem, recv_sem, 100,
+    shared_a = share(0)
+    value_grad(1, halo_b)
+    shared_b = share(1)
+    acts_in.wait_recv()
+    spread_out(other_acts, 1 - z)
+
+    shared_a.wait_recv()
+    for i in range(4):
+        block = jnp.dot(
+            acts_t[i * 384 : i * 384 + 384, :], dv_all[0], preferred_element_type=F32
+        ).reshape(2, NX, PAD, 128)
+        for t in range(NX):
+            gx[t, i // 2, i % 2 * 2 : i % 2 * 2 + 2] = block[:, t]
+    ring_x = Ring(
+        NX, x, lambda t, h: gx.at[t, h], rx, send_sem, recv_sem, 114,
+        lambda way: at_ctx(z, y, lax.rem(x + way + NX, NX)),
+    )
+    ring_x.step(0)
+
+    shared_b.wait_recv()
+    for i in range(2):
+        block = jnp.dot(
+            acts_t[i * 768 : i * 768 + 768, :], dv_all[1], preferred_element_type=F32
+        ).reshape(4, 2, 2, PAD, 128)
+        gy[i * 4 : i * 4 + 4] = block
+    ring_y = Ring(
+        NY, y, lambda t, h: gy.at[t, h], ry, send_sem, recv_sem, 100,
         lambda way: at_ctx(z, lax.rem(y + way + NY, NY), x),
     )
-    ring_a.step(0)
-    value_grad(1, halo_b)
-
-    def grad_b(i, carry):
-        for h in range(NZ):
-            rows = pl.ds(pl.multiple_of(h * 1536 + i * 384, 384), 384)
-            block = jnp.dot(acts_t[rows, :], dv_half[1], preferred_element_type=F32).reshape(
-                2, NX, PAD, 128
-            )
-            for t in range(NX):
-                gb[h, t, pl.ds(i * 2, 2)] = block[:, t]
-        return carry
-
-    lax.fori_loop(0, 4, grad_b, 0)
-    ring_b = Ring(
-        NX, x, lambda t, h: gb.at[h, t], rb, send_sem, recv_sem, 114,
-        lambda way: at_ctx(z, y, lax.rem(x + way + NX, NX)),
-    )
-    ring_b.step(0)
-    moments_forward()
-    ring_a.step(1)
+    ring_y.step(0)
+    moments_forward, moments_arrive = over_work(moments)
+    ring_x.step(1)
+    ring_y.step(1)
     for copy in whole_x:
         copy.wait_recv()
-    whole_z = send(whole.at[z], whole.at[z], at_ctx(1 - z, y, x))
-    ring_a.step(2)
-    ring_b.step(1)
-    ring_a.step(3)
-    ring_b.step(2)
-    ring_a.step(4)
-
+    rows_all = whole[...].reshape(HALF_PAD, KH * HD)
+    for owner in range(NZ):
+        part[owner] = lax.dot_general(
+            acts_t[:, owner * ROWS : owner * ROWS + ROWS],
+            rows_all,
+            (((0,), (0,)), ((), ())),
+            preferred_element_type=F32,
+        )
+    part_copy = send(part.at[1 - z], part_in, at_ctx(1 - z, y, x))
+    ring_y.step(2)
+    ring_x.step(2)
     second_a = []
-    for k in range(1, NZ * NX):
-        zz, xx = zx_peer(k)
-        second_a.append(send(ga.at[zz * NY + y, xx], ra2.at[k - 1], at_ctx(zz, y, xx)))
+    for k in range(1, NY):
+        yy = lax.rem(y + k, NY)
+        second_a.append(
+            send(gx.at[x, yy // 4, lax.rem(yy, 4)], rx2.at[k - 1], at_ctx(z, yy, x))
+        )
+    ring_y.step(3)
+    ring_y.step(4)
     second_b = []
-    for k in range(1, NZ * NY):
-        zz, yy = zy_peer(k)
-        second_b.append(send(gb.at[zz, x, yy], rb2.at[k - 1], at_ctx(zz, yy, x)))
-
-    whole_z.wait_recv()
-    values = lax.dot_general(
-        acts_t[...], whole[...].reshape(NCTX * PAD, KH * HD), (((0,), (0,)), ((), ())), preferred_element_type=F32
-    ).astype(BF16)
+    for k in range(1, NX):
+        xx = lax.rem(x + k, NX)
+        second_b.append(
+            send(gy.at[y, xx // 2, lax.rem(xx, 2)], ry2.at[k - 1], at_ctx(z, y, xx))
+        )
+
+    part_copy.wait_recv()
+    values = (part[z] + part_in[...]).astype(BF16)
     value_send[...] = values[ROWS - SPAN :]
     values_in = send(value_send, value_halo, {"ctx": nxt})
     widen(values, v2, SPAN, ROWS)
@@ -379,14 +392,14 @@
 
     for copy in second_a:
         copy.wait_recv()
-    half_a = ga[z * NY + y, x]
-    for k in range(1, NZ * NX):
-        half_a = half_a + ra2[k - 1]
+    half_a = gx[x, y // 4, lax.rem(y, 4)]
+    for k in range(1, NY):
+        half_a = half_a + rx2[k - 1]
     for copy in second_b:
         copy.wait_recv()
-    half_b = gb[z, x, y]
-    for k in range(1, NZ * NY):
-        half_b = half_b + rb2[k - 1]
+    half_b = gy[y, x // 2, lax.rem(x, 2)]
+    for k in range(1, NX):
+        half_b = half_b + ry2[k - 1]
     tokens_all = float(ROWS * NCTX)
     half_a, half_b = half_a / tokens_all, half_b / tokens_all
     grads[zh, core, :, :128] = half_a
@@ -407,6 +420,7 @@
         send(n_two_send, n_two.at[k - 1], at_ctx(z, lax.rem(y + k, NY), x)) for k in range(1, NY)
     ]
     grads_forward()
+    moments_forward()
     output(0)
     store = pltpu.make_async_copy(out, out_hbm, load_sem.at[9])
     store.start()
@@ -441,8 +455,8 @@
     store.wait()
     for copy in pending:
         copy.wait_send()
-    ring_a.finish()
-    ring_b.finish()
+    ring_x.finish()
+    ring_y.finish()
 
 
 def hand_over(*refs):
@@ -471,14 +485,14 @@
         out_specs=(hbm, vmem, vmem, vmem),
         scratch_shapes=[
             pltpu.VMEM((ROWS, QH * HD), BF16),
-            pltpu.VMEM((D, ROWS), BF16),
+            pltpu.VMEM((NZ, HALF, ROWS), BF16),
             pltpu.VMEM((ROWS, QH * HD), BF16),
             pltpu.VMEM((ROWS, width), BF16),
             pltpu.VMEM((ROWS, QH * HD), BF16),
             pltpu.VMEM((1, ROWS), jnp.int32),
             pltpu.VMEM((3, OWN, 1, width), F32),
             pltpu.VMEM((TILES, 128, 256), BF16),
-            pltpu.VMEM((NCTX * PAD, ROWS), BF16),
+            pltpu.VMEM((HALF_PAD, NZ * ROWS), BF16),
             pltpu.VMEM((KH, 2, SPAN + ROWS, 128), BF16),
             pltpu.VMEM((KH, 2, SPAN + ROWS, 128), BF16),
             pltpu.VMEM((2, KH, 2, ROWS, 512), BF16),
@@ -490,13 +504,17 @@
             pltpu.VMEM((SPAN, width), BF16),
             pltpu.VMEM((SPAN, width), BF16),
             pltpu.VMEM((SPAN, width), BF16),
-            pltpu.VMEM((NZ, NY, NX, PAD, width), BF16),
-            pltpu.VMEM((NZ * NY, NX, PAD, 128), F32),
-            pltpu.VMEM((NZ, NX, NY, PAD, 128), F32),
-            pltpu.VMEM((14, NX, PAD, 128), F32),
-            pltpu.VMEM((6, NY, PAD, 128), F32),
-            pltpu.VMEM((NZ * NX - 1, PAD, 128), F32),
-            pltpu.VMEM((NZ * NY - 1, PAD, 128), F32),
+            pltpu.VMEM((HALF, ROWS), BF16),
+            pltpu.VMEM((2, NZ * ROWS, 128), BF16),
+            pltpu.VMEM((NZ, ROWS, width), F32),
+            pltpu.VMEM((ROWS, width), F32),
+            pltpu.VMEM((NY, NX, PAD, width), BF16),
+            pltpu.VMEM((NX, 2, NY // 2, PAD, 128), F32),
+            pltpu.VMEM((NY, 2, NX // 2, PAD, 128), F32),
+            pltpu.VMEM((6, NY // 2, PAD, 128), F32),
+            pltpu.VMEM((14, NX // 2, PAD, 128), F32),
+            pltpu.VMEM((NY - 1, PAD, 128), F32),
+            pltpu.VMEM((NX - 1, PAD, 128), F32),
             pltpu.VMEM((NH, 2, 3, PAD, width), F32),
             pltpu.VMEM((NH, 2, PAD, width), F32),
             pltpu.VMEM((8, 128), F32),
@@ -513,7 +531,7 @@
         ),
         name="local_adam",
     )(
-        jnp.swapaxes(inputs[0], 0, 1), queries[0], keys[0], out_grad[0], positions, bands, step,
+        jnp.swapaxes(inputs[0], 0, 1).reshape(NZ, HALF, ROWS), queries[0], keys[0], out_grad[0], positions, bands, step,
         *[jnp.swapaxes(a, 0, 1) for a in (value_weight, moment_one, moment_two)], jnp.asarray(spread_matrix(), BF16),
     )
     results = (out, mean_weight, mean_one, mean_two)

time: 83.8 us -> 80 us (0.955)
  Pallas kernels: 82.4 us -> 78.6 us
    pallas_call x1, Pallas kernels: 80.1 us -> 76.3 us  [per_device(): pl.pallas_call(kernel, out_shape=(jax.ShapeDtypeStruct((ROWS, QH * HD), B...]
where the time goes in v3:
time: 80 us; the launch traced here: 79.9 us
  Pallas kernels  78.6 us (98%)
  between operations  1.29 us (2%)
    pallas_call x1, Pallas kernels, per_device(): pl.pallas_call(kernel, out_shape=(jax.ShapeDtypeStruct((ROWS, QH * HD), B...  76.3 us
    pallas_call x1, Pallas kernels, per_device(): pl.pallas_call(hand_over, out_shape=tuple((jax.ShapeDtypeStruct(a.shape,...  2.29 us

profile of v3, /device:TPU:1, one launch (start us, length us, event | category | flops | bytes accessed | tf_op | source)
XLA Modules:
  0.0 79.9 jit_solution(8080106299749515989)
XLA Ops:
  1.3 76.3 %local_adam.1 = (bf16[256,2048]{1,0:T(8,128)(2,1)}, f32[45,256]{1,0:T(8,128)}, f32[45,256]{1,0:T(8,128)}, f32[45,256]{1,0:T(8,128)}) custom-call(bf16[2,1440,256]{2,1,0:T(8,128)(2,1)} %bitcast.12, bf16[256,2048]{1,0:T(8,128)(2,1)} %bitcast.13, bf16[256,256]{1,0:T(8,128)(2,1)} %bitcast.15, bf16[256,2048]{1,0:T(8,128)(2,1)} %bitcast.14, ...), custom_call_target="tpu_custom_call" | custom-call | tf_op jit(solution)/shard_map/local_adam/pallas_call | solution.py:478
  77.6 2.3 %hand_over.1 = (bf16[256,2048]{1,0:T(8,128)(2,1)}, f32[45,256]{1,0:T(8,128)}, f32[45,256]{1,0:T(8,128)}, f32[45,256]{1,0:T(8,128)}) custom-call(bf16[256,2048]{1,0:T(8,128)(2,1)} %get-tuple-element.12.refs_0_, f32[45,256]{1,0:T(8,128)} %get-tuple-element.13.refs_1_, f32[45,256]{1,0:T(8,128)} %get-tuple-element.14.refs_2_, f32[45,256]{1,0:T(8,128)} %get-tuple-element.15.refs_3_), custom_call_target="tpu_custom_call" | custom-call | tf_op jit(solution)/shard_map/hand_over/pallas_call | solution.py:538

commit v4 on v3

--- a/solution.py
+++ b/solution.py
@@ -236,6 +236,11 @@
         dv_half[pair, :SPAN, :] = (first[SPAN:] + second[:SPAN]).astype(BF16)
         dv_half[pair, SPAN:, :] = (second[SPAN:] + dv_recv[pair]).astype(BF16)
 
+    pl.semaphore_wait(barrier, len(greeted))
+
+    keys_in = send(keys.at[pl.ds(ROWS - SPAN, SPAN)], key_halo, {"ctx": nxt})
+    loads[8].wait()
+    acts_in = send(acts.at[1 - z], other_acts, at_ctx(1 - z, y, x))
     for load in loads[2:4]:
         load.wait()
     attend(0, 1)
@@ -246,11 +251,6 @@
         moments[zh, core, index] = jnp.concatenate([state[index, :, 0, :], spare], 0)
     whole[y, x] = moments[zh, core, 0].astype(BF16)
 
-    pl.semaphore_wait(barrier, len(greeted))
-
-    keys_in = send(keys.at[pl.ds(ROWS - SPAN, SPAN)], key_halo, {"ctx": nxt})
-    loads[8].wait()
-    acts_in = send(acts.at[1 - z], other_acts, at_ctx(1 - z, y, x))
     whole_y = [send(whole.at[y, x], whole.at[y, x], at_ctx(z, lax.rem(y + k, NY), x)) for k in range(1, NY)]
 
     def over_work(buffer):
@@ -460,12 +460,24 @@
 
 
 def hand_over(*refs):
-    sems = refs[-1]
-    copies = [pltpu.make_async_copy(refs[i], refs[4 + i], sems.at[i]) for i in range(4)]
-    for copy in copies:
-        copy.start()
-    for copy in copies:
-        copy.wait()
+    sources, targets, held, load_sem, store_sem = refs[:4], refs[4:8], refs[8:12], refs[12], refs[13]
+    rows = ROWS // 4
+    parts = [(0, pl.ds(k * rows, rows)) for k in range(4)] + [(n, pl.ds(0, OWN)) for n in (1, 2, 3)]
+    loads = [
+        pltpu.make_async_copy(sources[n].at[at], held[n].at[at], load_sem.at[k])
+        for k, (n, at) in enumerate(parts)
+    ]
+    stores = [
+        pltpu.make_async_copy(held[n].at[at], targets[n].at[at], store_sem.at[k])
+        for k, (n, at) in enumerate(parts)
+    ]
+    for load in loads:
+        load.start()
+    for load, store in zip(loads, stores):
+        load.wait()
+        store.start()
+    for store in stores:
+        store.wait()
 
 
 def per_device(
@@ -538,9 +550,13 @@
     out, mean_weight, mean_one, mean_two = pl.pallas_call(
         hand_over,
         out_shape=tuple(jax.ShapeDtypeStruct(a.shape, a.dtype) for a in results),
-        in_specs=[vmem] * 4,
+        in_specs=[hbm] * 4,
         out_specs=(hbm,) * 4,
-        scratch_shapes=[pltpu.SemaphoreType.DMA((4,))],
+        scratch_shapes=[
+            *[pltpu.VMEM(a.shape, a.dtype) for a in results],
+            pltpu.SemaphoreType.DMA((7,)),
+            pltpu.SemaphoreType.DMA((7,)),
+        ],
         name="hand_over",
     )(*results)
     return out[None], mean_weight, mean_one, mean_two

time: 80 us -> 80.3 us (level)
  no operation moved by 1% of the time
where the time goes in v4:
time: 80.3 us; the launch traced here: 80.1 us
  Pallas kernels  78.8 us (98%)
  between operations  1.29 us (2%)
    pallas_call x1, Pallas kernels, per_device(): pl.pallas_call(kernel, out_shape=(jax.ShapeDtypeStruct((ROWS, QH * HD), B...  76.7 us
    pallas_call x1, Pallas kernels, per_device(): pl.pallas_call(hand_over, out_shape=tuple((jax.ShapeDtypeStruct(a.shape,...  2.07 us

profile of v4, /device:TPU:1, one launch (start us, length us, event | category | flops | bytes accessed | tf_op | source)
XLA Modules:
  0.0 80.1 jit_solution(4874070453907873281)
XLA Ops:
  1.3 76.7 %local_adam.1 = (bf16[256,2048]{1,0:T(8,128)(2,1)}, f32[45,256]{1,0:T(8,128)}, f32[45,256]{1,0:T(8,128)}, f32[45,256]{1,0:T(8,128)}) custom-call(bf16[2,1440,256]{2,1,0:T(8,128)(2,1)} %bitcast.12, bf16[256,2048]{1,0:T(8,128)(2,1)} %bitcast.13, bf16[256,256]{1,0:T(8,128)(2,1)} %bitcast.15, bf16[256,2048]{1,0:T(8,128)(2,1)} %bitcast.14, ...), custom_call_target="tpu_custom_call" | custom-call | tf_op jit(solution)/shard_map/local_adam/pallas_call | solution.py:490
  78.0 2.1 %hand_over.1 = (bf16[256,2048]{1,0:T(8,128)(2,1)}, f32[45,256]{1,0:T(8,128)}, f32[45,256]{1,0:T(8,128)}, f32[45,256]{1,0:T(8,128)}) custom-call(bf16[256,2048]{1,0:T(8,128)(2,1)} %get-tuple-element.12.refs_0_, f32[45,256]{1,0:T(8,128)} %get-tuple-element.13.refs_1_, f32[45,256]{1,0:T(8,128)} %get-tuple-element.14.refs_2_, f32[45,256]{1,0:T(8,128)} %get-tuple-element.15.refs_3_), custom_call_target="tpu_custom_call" | custom-call | tf_op jit(solution)/shard_map/hand_over/pallas_call | solution.py:550
